TPU v7x, 32 devices: a whole 2x2x4 slice. The times are simulated.
32 devices in a mesh: ka: 16 (over z, y, core), pa: 2 (over x).
Axes of the slice: x: 2, y: 2, z: 4, core: 2. Of those that a mesh axis runs over, the one named last changes fastest.
Arguments:
- conduction: bfloat16 [16, 48, 2048], P('ka'), may hold values from -6 to 6
- weighted: bfloat16 [16, 48, 2048], P('ka'), may hold values from -6 to 6
- valence: bfloat16 [16, 64, 2048], P('ka', None, 'pa'), may hold values from -0.03125 to 0.03125
- screening: bfloat16 [16, 2048, 2048], P('ka', None, 'pa'), may hold values from -0.125 to 0.125
- pair_transfer: int32 [16, 16], replicated, may hold values from 0 to 15, as said below
- owner_map: int32 [16], replicated, may hold values from 0 to 15, each once
Outputs:
- kernel_out: float32 [16, 48, 64], P('ka')
Inputs may be any that keep to these rules, and one draw needn't show every extreme that they name: pair_transfer[i, j] = (g_i - g_j) mod 16 for positions g of the k-points on a cyclic grid of 16 points (a permutation drawn from the seed), so each row and each column names every transfer once. `owner_map`: each transfer is held by exactly one slot.
All inputs are finite; a program needn't handle non-finite values.
Results may differ from a plain program's by a relative error of at most 0.0029.
Values may be sent and summed in bfloat16 or wider, within the bound.
A program may use at most 128 MiB of HBM per device.

v0:
```python
import jax
import jax.numpy as jnp
from jax import lax
from jax.sharding import PartitionSpec as P


def shards(conduction, weighted, valence, screening, pair_transfer, owner_map):
    local_count = conduction.shape[0]
    half_width = screening.shape[2]
    first_column = lax.axis_index("pa") * half_width
    first_slot = lax.axis_index("ka") * local_count
    owned_transfers = lax.dynamic_slice_in_dim(owner_map, first_slot, local_count)
    columns = jnp.arange(pair_transfer.shape[1], dtype=jnp.int32)
    matches = pair_transfer[None, :, :] == owned_transfers[:, None, None]
    partners = jnp.sum(jnp.where(matches, columns[None, None, :], 0), axis=2)
    every_cond = lax.all_gather(conduction, "ka", axis=0, tiled=True)
    piece = lax.all_gather(weighted, "ka", axis=0, tiled=True)
    count = piece.shape[0]
    total = jnp.zeros((count, piece.shape[1], half_width), jnp.float32)
    partner_rows = partners[0]
    partner_cond = jnp.take(every_cond, partner_rows, axis=0)
    density = (partner_cond.astype(jnp.float32) * piece.astype(jnp.float32)).astype(jnp.bfloat16)
    screened = jnp.dot(
        density.reshape(-1, density.shape[2]), screening[0], preferred_element_type=jnp.float32
    )
    partner_half = lax.dynamic_slice_in_dim(partner_cond, first_column, half_width, 2)
    total = partner_half.astype(jnp.float32) * screened.reshape(total.shape)
    folded = lax.psum_scatter(total, "ka", scatter_dimension=0, tiled=True)
    partial_out = jnp.einsum(
        "kbp,kvp->kbv", folded, valence.astype(jnp.float32), precision=lax.Precision.HIGHEST
    )
    return lax.psum(partial_out, "pa")


def solution(mesh):
    in_specs = (
        P("ka", None, None),
        P("ka", None, None),
        P("ka", None, "pa"),
        P("ka", None, "pa"),
        P(),
        P(),
    )
    out_specs = P("ka", None, None)
    return jax.shard_map(shards, mesh=mesh, in_specs=in_specs, out_specs=out_specs, check_vma=False)
```

profile of v0, /device:TPU:0, one launch (start us, length us, event | category | flops | bytes accessed | tf_op | source)
XLA Modules:
  0.0 195.3 jit_solution(1086610348738875240)
XLA Ops:
  6.5 0.0 copy-start
  6.5 0.0 all-gather.3.cloned.1.call-start
  6.5 0.7 all-gather.3.cloned.1.call-update
  7.3 0.0 all-gather.5.cloned.1.call-start
  7.3 0.7 all-gather.5.cloned.1.call-update
  8.0 0.0 reduce-scatter.2.cloned.1.call-start
  8.1 1.2 dynamic_slice.6
  9.3 1.5 select_reduce_fusion
  10.8 46.8 %all-gather.3.cloned.1.call-done = bf16[16,48,2048]{2,1,0:T(8,128)(2,1)} async-done(((bf16[1,48,2048]{2,1,0:T(8,128)(2,1)}), bf16[16,48,2048]{2,1,0:T(8,128)(2,1)}) %all-gather.3.cloned.1.call-update) | async-done | bytes 3145744 | tf_op jit(solution)/shard_map/all_gather | solution.py:16
  57.6 2.6 %gather_fusion = bf16[16,48,2048]{2,1,0:T(8,128)(2,1)S(1)} fusion(bf16[16,48,2048]{2,1,0:T(8,128)(2,1)} %all-gather.3.cloned.1.call-done, s32[1024]{0:T(1024)S(1)} %pad_clamp_fusion), kind=kCustom, calls=%fused_computation | custom fusion | bytes 6291520 | tf_op jit(solution)/shard_map/jit(_take)/gather | solution.py:21
  60.2 2.1 %broadcast_select_fusion = bf16[16,48,2048]{2,1,0:T(8,128)(2,1)} fusion(bf16[16,48,2048]{2,1,0:T(8,128)(2,1)S(1)} %gather_fusion, pred[16]{0:T(512)(128)(4,1)S(1)} %compare_and_fusion), kind=kLoop, calls=%fused_computation.5 | loop fusion | flops 1572864 | bytes 6291472 | tf_op jit(solution)/shard_map/jit(_take)/select_n | solution.py:21
  62.3 41.6 %all-gather.5.cloned.1.call-done = bf16[16,48,2048]{2,1,0:T(8,128)(2,1)} async-done(((bf16[1,48,2048]{2,1,0:T(8,128)(2,1)}), bf16[16,48,2048]{2,1,0:T(8,128)(2,1)}) %all-gather.5.cloned.1.call-update) | async-done | bytes 3145744 | tf_op jit(solution)/shard_map/all_gather | solution.py:17
  103.9 9.6 %convert_multiply_fusion = f32[16,48,1024]{2,1,0:T(8,128)} fusion(bf16[1,2048,1024]{2,1,0:T(8,128)(2,1)} %param.9, bf16[16,48,2048]{2,1,0:T(8,128)(2,1)} %all-gather.5.cloned.1.call-done, bf16[16,48,2048]{2,1,0:T(8,128)(2,1)} %broadcast_select_fusion, s32[]{:T(128)S(6)} %select_n.36), kind=kOutput, calls=%fused_computation.4 | convolution fusion | flops 3229089792 | bytes 15204356 | tf_op jit(solution)/shard_map/dot_general | solution.py:23
  113.5 0.0 reduce-scatter.2.cloned.1.call-update
  113.5 65.2 %reduce-scatter.2.cloned.1.call-done = f32[1,48,1024]{2,1,0:T(8,128)} async-done(((f32[16,48,1024]{2,1,0:T(8,128)}), f32[1,48,1024]{2,1,0:T(8,128)}) %reduce-scatter.2.cloned.1.call-update) | async-done | bytes 196624 | tf_op jit(solution)/shard_map/reduce_scatter | solution.py:28
  178.7 0.0 copy-done
  178.7 1.2 convolution_bitcast_fusion
  179.9 8.9 %psum.7 = f32[1,48,64]{2,1,0:T(8,128)} all-reduce(f32[1,48,64]{2,1,0:T(8,128)S(1)} %convolution_bitcast_fusion), channel_id=1, replica_groups=mesh['ka'=16,'pa'=2] {'pa'}, use_global_device_ids=true, to_apply=%region_2.3 | all-reduce | flops 3072 | bytes 24576 | tf_op jit(solution)/shard_map/psum | solution.py:32
  (3 shorter events, 0.0 us)
Async XLA Ops:
  6.5 172.2 %copy-start = (bf16[1,64,1024]{2,1,0:T(8,128)(2,1)S(1)}, bf16[1,64,1024]{2,1,0:T(8,128)(2,1)}, u32[]{:S(2)}) copy-start(bf16[1,64,1024]{2,1,0:T(8,128)(2,1)} %param.8) | copy-start | bytes 393220
  6.5 51.0 %all-gather.3.cloned.1.call-start = ((), (), s32[]{:S(2)}) async-start(), calls=%async_computation.1 | async-start | bytes 3342336 | tf_op jit(solution)/shard_map/all_gather | solution.py:16
  7.3 96.6 %all-gather.5.cloned.1.call-start = ((), (), s32[]{:S(2)}) async-start(), calls=%async_computation.2 | async-start | bytes 3342336 | tf_op jit(solution)/shard_map/all_gather | solution.py:17
  8.0 170.7 %reduce-scatter.2.cloned.1.call-start = ((), (), s32[]{:S(2)}) async-start(), calls=%async_computation.3 | async-start | bytes 3342336 | tf_op jit(solution)/shard_map/reduce_scatter | solution.py:28
Sparse Core Ops, SparseCore 0:
  9.6 47.8 all-gather.2
  59.8 43.9 all-gather.4
  113.6 65.0 reduce-scatter.1
where the time goes:
time: 196 us; the launch traced here: 195 us
  waiting for transfers between devices  155 us (79%)
  between operations  13.1 us (7%)
  matrix products  10.8 us (6%)
  blocking collectives  8.87 us (5%)
  local copies, waits for them, and re-layouts  3.88 us (2%)
  other arithmetic  3.53 us (2%)
    reduce_scatter x1, waiting for transfers between devices, shards(): folded = lax.psum_scatter(total, 'ka', scatter_dimension=0, tiled=True)  65.2 us
    all_gather x1, waiting for transfers between devices, shards(): every_cond = lax.all_gather(conduction, 'ka', axis=0, tiled=True)  46.8 us
    all_gather x1, waiting for transfers between devices, shards(): piece = lax.all_gather(weighted, 'ka', axis=0, tiled=True)  41.6 us
    dot_general x1, matrix products, shards(): jnp.dot(density.reshape(-1, density.shape[2]), screening[0], preferred_el...  9.6 us
    psum x1, blocking collectives, shards(): return lax.psum(partial_out, 'pa')  8.87 us
  transfers between devices with their start and end apart: 3, of which 3 were waited for; matrix products, arithmetic and copies ran while one was open for 4% of the time, Pallas kernels for 0%

commit v1 on v0

v1 whole, which is shorter than its diff:
```python
import functools

import jax
import jax.numpy as jnp
from jax import lax
from jax.experimental import pallas as pl
from jax.experimental.pallas import tpu as pltpu
from jax.sharding import PartitionSpec as P

MESH = pl.DeviceIdType.MESH
TILE = 256


def kernel(
    nk, halves, pair_ref, owner_ref, cond_ref, wt_ref, val_ref, scr_ref, out_ref,
    cond_all, wt_all, val_all, scr, dens, acc, given, taken, partner,
    own_sem, scr_sem, z_send, z_recv, y_send, y_recv, x_send, x_recv, c_send, c_recv,
    end_send, end_recv,
):
    nb, half = cond_all.shape[2], cond_all.shape[3]
    nv = val_all.shape[1]
    n = nk // 4
    ka = lax.axis_index("ka")
    pa = lax.axis_index("pa")
    core = lax.rem(ka, 2)
    mid = lax.rem(ka // 2, 2)
    outer = ka // 4
    devices = nk * halves
    me = ka * halves + pa

    def point(o, m, c):
        return (o * 2 + m) * 2 + c

    upper = (2 * outer) // n
    shorter = outer * (1 - upper) + (n - 1 - outer) * upper

    def layer(t):
        near = (2 * lax.rem(t, 2) - 1) * ((t + 1) // 2)
        far = (1 - 2 * upper) * (t - shorter)
        beyond = (t - 1 - 2 * shorter + 2 * n) // (2 * n)
        return outer + near * (1 - beyond) + far * beyond

    own = []
    for h in range(halves):
        own.append(pltpu.make_async_copy(cond_ref.at[0, :, pl.ds(h * half, half)], cond_all.at[ka, h], own_sem.at[0, h]))
        own.append(pltpu.make_async_copy(wt_ref.at[0, :, pl.ds(h * half, half)], wt_all.at[ka, h], own_sem.at[1, h]))
    own.append(pltpu.make_async_copy(val_ref.at[0], val_all.at[ka], own_sem.at[2, 0]))
    for copy in own:
        copy.start()
    scr_copy = pltpu.make_async_copy(scr_ref.at[0], scr, scr_sem.at[0])
    scr_copy.start()

    barrier = pltpu.get_barrier_semaphore()

    @pl.loop(1, devices)
    def _(d):
        other = lax.rem(me + d, devices)
        pl.semaphore_signal(barrier, inc=1, device_id=(other // halves, lax.rem(other, halves)), device_id_type=MESH)

    pl.semaphore_wait(barrier, devices - 1)
    for copy in own:
        copy.wait()
    scr_copy.wait()

    def block(kind, o, m, c, h):
        if kind == 2:
            return val_all.at[point(o, m, c)]
        return (cond_all, wt_all)[kind].at[point(o, m, c), h]

    def remote(ref, send, recv, device):
        return pltpu.make_async_remote_copy(
            src_ref=ref, dst_ref=ref, send_sem=send, recv_sem=recv, device_id=device, device_id_type=MESH
        )

    def z_copy(kind, o, way):
        to = lax.rem(outer + (1 if way else n - 1), n)
        return remote(
            block(kind, o, mid, core, pa), z_send.at[kind, way, o], z_recv.at[kind, o], (point(to, mid, core), pa)
        )

    def y_copy(kind, o, m):
        return remote(
            block(kind, o, m, core, pa), y_send.at[kind, o], y_recv.at[kind, o], (point(outer, 1 - mid, core), pa)
        )

    def x_copy(kind, o, m, h):
        return remote(
            block(kind, o, m, core, h), x_send.at[kind, o, m], x_recv.at[kind, o, m], (ka, 1 - pa)
        )

    def c_copy(kind, o, m, c, h):
        slot = 0 if kind == 2 else h
        return remote(
            block(kind, o, m, c, h), c_send.at[kind, o, m, slot], c_recv.at[kind, o, m, slot],
            (point(outer, mid, 1 - core), pa),
        )

    def stage_a(kind, t):
        o = layer(t)

        @pl.when(t > 0)
        def _():
            z_copy(kind, o, 0).wait_recv()

        @pl.when((o <= outer) & (outer < n - 1))
        def _():
            z_copy(kind, o, 1).start()

        @pl.when((o >= outer) & (outer > 0))
        def _():
            z_copy(kind, o, 0).start()

        y_copy(kind, o, mid).start()
        if kind < 2:
            @pl.when(t > 0)
            def _():
                x_copy(kind, o, mid, pa).start()
        c_copy(kind, o, mid, core, pa).start()

    def stage_b(kind, t):
        o = layer(t)
        y_copy(kind, o, 1 - mid).wait_recv()
        if kind < 2:
            x_copy(kind, o, 1 - mid, pa).start()
        c_copy(kind, o, 1 - mid, core, pa).start()

    def stage_c(kind, t):
        if kind < 2:
            o = layer(t)
            for m in (mid, 1 - mid):
                @pl.when((t > 0) | (m != mid))
                def _():
                    x_copy(kind, o, m, 1 - pa).wait_recv()

                c_copy(kind, o, m, core, 1 - pa).start()

    def stage_d(kind, t):
        o = layer(t)
        for m in range(2):
            for h in range(1 if kind == 2 else halves):
                c_copy(kind, o, m, 1 - core, h).wait_recv()

    def end_copy(k, h):
        return pltpu.make_async_remote_copy(
            src_ref=given.at[k], dst_ref=taken.at[me], send_sem=end_send.at[k, h], recv_sem=end_recv.at[me],
            device_id=(k, h), device_id_type=MESH,
        )

    def compute(o):
        for q in range(4):
            k = o * 4 + q
            for h in range(halves):
                dens[q * nb:(q + 1) * nb, h * half:(h + 1) * half] = cond_all[partner[k], h] * wt_all[k, h]
        total = None
        for lo in range(0, half, TILE):
            cols = slice(lo, lo + TILE)
            screened = jnp.dot(dens[...], scr[:, cols], preferred_element_type=jnp.float32)
            terms = jnp.concatenate(
                [
                    (cond_all[partner[o * 4 + q], pa, :, cols].astype(jnp.float32) * screened[q * nb:(q + 1) * nb])
                    .astype(jnp.bfloat16)
                    for q in range(4)
                ],
                axis=0,
            )
            val = jnp.concatenate([val_all[o * 4 + q, :, cols] for q in range(4)], axis=0)
            part = lax.dot_general(terms, val, (((1,), (1,)), ((), ())), preferred_element_type=jnp.float32)
            total = part if total is None else total + part
        acc[...] = total

        first = lax.broadcasted_iota(jnp.int32, (nb // 2, 2 * nv), 1) < nv
        for q in range(4):
            k = o * 4 + q
            lanes = slice((q // 2) * 2 * nv, (q // 2 + 1) * 2 * nv)
            top = acc[q * nb:q * nb + nb // 2, lanes]
            low = acc[q * nb + nb // 2:(q + 1) * nb, lanes]
            if q % 2 == 0:
                packed = jnp.where(first, top, pltpu.roll(low, nv, 1))
            else:
                packed = jnp.where(first, pltpu.roll(top, nv, 1), low)
            given[k] = packed

    def staged(stage, u):
        @pl.when((u >= 0) & (u < n))
        def _():
            stage(0, u)

        @pl.when((u >= n) & (u < 2 * n))
        def _():
            stage(1, u - n)
            stage(2, u - n)

    @pl.loop(0, 2 * n + 3)
    def _(u):
        staged(stage_a, u)
        staged(stage_b, u - 1)
        staged(stage_c, u - 2)
        staged(stage_d, u - 3)

        @pl.when(u == 0)
        def _():
            held = owner_ref[ka]

            @pl.loop(0, nk)
            def _(i):
                partner[i] = lax.fori_loop(
                    0, nk, lambda j, found: jnp.where(pair_ref[i, j] == held, j, found), jnp.int32(0)
                )

    @pl.loop(0, n)
    def _(o):
        compute(o)

    @pl.loop(1, devices)
    def _(d):
        other = lax.rem(me + d, devices)
        end_copy(other // halves, lax.rem(other, halves)).start()

    @pl.loop(0, n)
    def _(o):
        for kind in range(3):
            @pl.when((o <= outer) & (outer < n - 1))
            def _():
                z_copy(kind, o, 1).wait_send()

            @pl.when((o >= outer) & (outer > 0))
            def _():
                z_copy(kind, o, 0).wait_send()

            y_copy(kind, o, mid).wait_send()
            for m in range(2):
                if kind < 2:
                    @pl.when((o != outer) | (m != mid))
                    def _():
                        x_copy(kind, o, m, pa).wait_send()

                for h in range(1 if kind == 2 else halves):
                    c_copy(kind, o, m, core, h).wait_send()

    @pl.loop(0, devices)
    def _(d):
        k, h = d // halves, lax.rem(d, halves)

        @pl.when(d != me)
        def _():
            end_copy(k, h).wait_send()
            pltpu.make_async_remote_copy(
                src_ref=given.at[k], dst_ref=taken.at[d], send_sem=end_send.at[k, h], recv_sem=end_recv.at[d],
                device_id=(k, h), device_id_type=MESH,
            ).wait_recv()

    total = lax.fori_loop(1, devices, lambda d, s: s + taken[lax.rem(me + d, devices)], given[ka])
    out_ref[0, :nb // 2, :] = total[:, :nv]
    out_ref[0, nb // 2:, :] = pltpu.roll(total, nv, 1)[:, :nv]


def shards(nk, halves, conduction, weighted, valence, screening, pair_transfer, owner_map):
    nb, width = conduction.shape[1:]
    nv, half = valence.shape[1:]
    n = nk // 4
    devices = nk * halves
    bf16, f32 = jnp.bfloat16, jnp.float32
    dma = pltpu.SemaphoreType.DMA
    smem = pl.BlockSpec(memory_space=pltpu.SMEM)
    anywhere = pl.BlockSpec(memory_space=pl.ANY)
    return pl.pallas_call(
        functools.partial(kernel, nk, halves),
        out_shape=jax.ShapeDtypeStruct((1, nb, nv), f32),
        in_specs=[smem, smem, anywhere, anywhere, anywhere, anywhere],
        out_specs=pl.BlockSpec(memory_space=pltpu.VMEM),
        scratch_shapes=[
            pltpu.VMEM((nk, halves, nb, half), bf16),
            pltpu.VMEM((nk, halves, nb, half), bf16),
            pltpu.VMEM((nk, nv, half), bf16),
            pltpu.VMEM((width, half), bf16),
            pltpu.VMEM((4 * nb, width), bf16),
            pltpu.VMEM((4 * nb, 4 * nv), f32),
            pltpu.VMEM((nk, nb // 2, 2 * nv), f32),
            pltpu.VMEM((devices, nb // 2, 2 * nv), f32),
            pltpu.SMEM((nk,), jnp.int32),
            dma((3, halves)),
            dma((1,)),
            dma((3, 2, n)),
            dma((3, n)),
            dma((3, n)),
            dma((3, n)),
            dma((2, n, 2)),
            dma((2, n, 2)),
            dma((3, n, 2, halves)),
            dma((3, n, 2, halves)),
            dma((nk, halves)),
            dma((devices,)),
        ],
        compiler_params=pltpu.CompilerParams(
            collective_id=0, has_side_effects=True, vmem_limit_bytes=56 * 1024 * 1024
        ),
    )(pair_transfer, owner_map, conduction, weighted, valence, screening)


def solution(mesh):
    in_specs = (
        P("ka", None, None),
        P("ka", None, None),
        P("ka", None, "pa"),
        P("ka", None, "pa"),
        P(),
        P(),
    )
    body = functools.partial(shards, mesh.shape["ka"], mesh.shape["pa"])
    return jax.shard_map(body, mesh=mesh, in_specs=in_specs, out_specs=P("ka", None, None), check_vma=False)
```

time: 196 us -> 66.2 us (0.34)
  the two profiles are of different devices: /device:TPU:0 before, /device:TPU:13 now
where the time goes in v1:
time: 66.2 us; the launch traced here: 66 us
  Pallas kernels  64.6 us (98%)
  local copies, waits for them, and re-layouts  1.35 us (2%)
    pallas_call x1, Pallas kernels, shards(): pl.pallas_call(functools.partial(kernel, nk, halves), out_shape=jax.Shape...  64.6 us
    unnamed x1, local copies, waits for them, and re-layouts  1.35 us

profile of v1, /device:TPU:13, one launch (start us, length us, event | category | flops | bytes accessed | tf_op | source)
XLA Modules:
  0.0 66.0 jit_solution(13124002508177395800)
XLA Ops:
  0.0 64.6 %shard_map.64 = f32[1,48,64]{2,1,0:T(8,128)} custom-call(s32[16,16]{1,0:T(8,128)} %pair_ref.1, s32[16]{0:T(128)} %owner_ref.1, bf16[1,48,2048]{2,1,0:T(8,128)(2,1)} %cond_ref.1, bf16[1,48,2048]{2,1,0:T(8,128)(2,1)} %wt_ref.1, bf16[1,64,1024]{2,1,0:T(8,128)(2,1)} %val_ref.1, bf16[1,2048,1024]{2,1,0:T(8,128)(2,1)} %scr_ref.1), custom_call_target="tpu_custom_call" | custom-call | tf_op jit(solution)/shard_map/pallas_call | solution.py:266
  64.6 1.3 %copy.8 = f32[1,48,64]{2,1,0:T(8,128)} copy(f32[1,48,64]{2,1,0:T(8,128)} %shard_map.64) | data formatting | bytes 24576

commit v2 on v1

--- a/solution.py
+++ b/solution.py
@@ -13,7 +13,7 @@
 
 def kernel(
     nk, halves, pair_ref, owner_ref, cond_ref, wt_ref, val_ref, scr_ref, out_ref,
-    cond_all, wt_all, val_all, scr, dens, acc, given, taken, partner,
+    cond_all, wt_all, val_all, scr, dens, terms, acc, given, taken, partner,
     own_sem, scr_sem, z_send, z_recv, y_send, y_recv, x_send, x_recv, c_send, c_recv,
     end_send, end_recv,
 ):
@@ -146,28 +146,23 @@
             device_id=(k, h), device_id_type=MESH,
         )
 
-    def compute(o):
+    def fold(o):
         for q in range(4):
             k = o * 4 + q
             for h in range(halves):
                 dens[q * nb:(q + 1) * nb, h * half:(h + 1) * half] = cond_all[partner[k], h] * wt_all[k, h]
-        total = None
         for lo in range(0, half, TILE):
             cols = slice(lo, lo + TILE)
             screened = jnp.dot(dens[...], scr[:, cols], preferred_element_type=jnp.float32)
-            terms = jnp.concatenate(
-                [
-                    (cond_all[partner[o * 4 + q], pa, :, cols].astype(jnp.float32) * screened[q * nb:(q + 1) * nb])
-                    .astype(jnp.bfloat16)
-                    for q in range(4)
-                ],
-                axis=0,
-            )
-            val = jnp.concatenate([val_all[o * 4 + q, :, cols] for q in range(4)], axis=0)
-            part = lax.dot_general(terms, val, (((1,), (1,)), ((), ())), preferred_element_type=jnp.float32)
-            total = part if total is None else total + part
-        acc[...] = total
-
+            for q in range(4):
+                k = o * 4 + q
+                terms[o, q * nb:(q + 1) * nb, cols] = (
+                    cond_all[partner[k], pa, :, cols].astype(jnp.float32) * screened[q * nb:(q + 1) * nb]
+                ).astype(jnp.bfloat16)
+
+    def contract(o):
+        val = jnp.concatenate([val_all[o * 4 + q] for q in range(4)], axis=0)
+        acc[...] = lax.dot_general(terms[o], val, (((1,), (1,)), ((), ())), preferred_element_type=jnp.float32)
         first = lax.broadcasted_iota(jnp.int32, (nb // 2, 2 * nv), 1) < nv
         for q in range(4):
             k = o * 4 + q
@@ -188,9 +183,12 @@
         @pl.when((u >= n) & (u < 2 * n))
         def _():
             stage(1, u - n)
-            stage(2, u - n)
-
-    @pl.loop(0, 2 * n + 3)
+
+        @pl.when((u >= 2 * n) & (u < 3 * n))
+        def _():
+            stage(2, u - 2 * n)
+
+    @pl.loop(0, 3 * n + 3)
     def _(u):
         staged(stage_a, u)
         staged(stage_b, u - 1)
@@ -207,9 +205,13 @@
                     0, nk, lambda j, found: jnp.where(pair_ref[i, j] == held, j, found), jnp.int32(0)
                 )
 
+        @pl.when(u >= 2 * n + 3)
+        def _():
+            fold(u - 2 * n - 3)
+
     @pl.loop(0, n)
     def _(o):
-        compute(o)
+        contract(o)
 
     @pl.loop(1, devices)
     def _(d):
@@ -274,6 +276,7 @@
             pltpu.VMEM((nk, nv, half), bf16),
             pltpu.VMEM((width, half), bf16),
             pltpu.VMEM((4 * nb, width), bf16),
+            pltpu.VMEM((n, 4 * nb, half), bf16),
             pltpu.VMEM((4 * nb, 4 * nv), f32),
             pltpu.VMEM((nk, nb // 2, 2 * nv), f32),
             pltpu.VMEM((devices, nb // 2, 2 * nv), f32),

time: 66.2 us -> 70.4 us (1.063)
  the two profiles are of different devices: /device:TPU:13 before, /device:TPU:0 now
where the time goes in v2:
time: 70.4 us; the launch traced here: 70.2 us
  Pallas kernels  68.8 us (98%)
  local copies, waits for them, and re-layouts  1.35 us (2%)
    pallas_call x1, Pallas kernels, shards(): pl.pallas_call(functools.partial(kernel, nk, halves), out_shape=jax.Shape...  68.8 us

profile of v2, /device:TPU:0, one launch (start us, length us, event | category | flops | bytes accessed | tf_op | source)
XLA Modules:
  0.0 70.2 jit_solution(10364793269694376982)
XLA Ops:
  0.0 68.8 %shard_map.64 = f32[1,48,64]{2,1,0:T(8,128)} custom-call(s32[16,16]{1,0:T(8,128)} %pair_ref.1, s32[16]{0:T(128)} %owner_ref.1, bf16[1,48,2048]{2,1,0:T(8,128)(2,1)} %cond_ref.1, bf16[1,48,2048]{2,1,0:T(8,128)(2,1)} %wt_ref.1, bf16[1,64,1024]{2,1,0:T(8,128)(2,1)} %val_ref.1, bf16[1,2048,1024]{2,1,0:T(8,128)(2,1)} %scr_ref.1), custom_call_target="tpu_custom_call" | custom-call | tf_op jit(solution)/shard_map/pallas_call | solution.py:268
  68.8 1.3 %copy.8 = f32[1,48,64]{2,1,0:T(8,128)} copy(f32[1,48,64]{2,1,0:T(8,128)} %shard_map.64) | data formatting | bytes 24576

commit v3 on v2

--- a/solution.py
+++ b/solution.py
@@ -184,15 +184,18 @@
         def _():
             stage(1, u - n)
 
-        @pl.when((u >= 2 * n) & (u < 3 * n))
-        def _():
-            stage(2, u - 2 * n)
-
-    @pl.loop(0, 3 * n + 3)
+    def valence_staged(stage, u):
+        @pl.when((u >= n) & (u < 2 * n))
+        def _():
+            stage(2, u - n)
+
+    @pl.loop(0, 2 * n + 3)
     def _(u):
         staged(stage_a, u)
         staged(stage_b, u - 1)
+        valence_staged(stage_a, u - 1)
         staged(stage_c, u - 2)
+        valence_staged(stage_b, u - 2)
         staged(stage_d, u - 3)
 
         @pl.when(u == 0)
@@ -205,9 +208,13 @@
                     0, nk, lambda j, found: jnp.where(pair_ref[i, j] == held, j, found), jnp.int32(0)
                 )
 
-        @pl.when(u >= 2 * n + 3)
-        def _():
-            fold(u - 2 * n - 3)
+    @pl.loop(0, n)
+    def _(o):
+        fold(o)
+
+    @pl.loop(0, n)
+    def _(t):
+        stage_d(2, t)
 
     @pl.loop(0, n)
     def _(o):

time: 70.4 us -> 64.4 us (0.915); the launches traced: 70.2 us -> 63.4 us
  Pallas kernels: 68.8 us -> 62 us
    pallas_call x1, Pallas kernels: 68.8 us -> 62 us  [shards(): pl.pallas_call(functools.partial(kernel, nk, halves), out_shape=jax.Shape...]
where the time goes in v3:
time: 64.4 us; the launch traced here: 63.4 us
  Pallas kernels  62 us (96%)
  local copies, waits for them, and re-layouts  1.35 us (2%)
    pallas_call x1, Pallas kernels, shards(): pl.pallas_call(functools.partial(kernel, nk, halves), out_shape=jax.Shape...  62 us
    unnamed x1, local copies, waits for them, and re-layouts  1.35 us

profile of v3, /device:TPU:0, one launch (start us, length us, event | category | flops | bytes accessed | tf_op | source)
XLA Modules:
  0.0 63.4 jit_solution(11655615879635491258)
XLA Ops:
  0.0 62.0 %shard_map.64 = f32[1,48,64]{2,1,0:T(8,128)} custom-call(s32[16,16]{1,0:T(8,128)} %pair_ref.1, s32[16]{0:T(128)} %owner_ref.1, bf16[1,48,2048]{2,1,0:T(8,128)(2,1)} %cond_ref.1, bf16[1,48,2048]{2,1,0:T(8,128)(2,1)} %wt_ref.1, bf16[1,64,1024]{2,1,0:T(8,128)(2,1)} %val_ref.1, bf16[1,2048,1024]{2,1,0:T(8,128)(2,1)} %scr_ref.1), custom_call_target="tpu_custom_call" | custom-call | tf_op jit(solution)/shard_map/pallas_call | solution.py:275
  62.1 1.3 %copy.8 = f32[1,48,64]{2,1,0:T(8,128)} copy(f32[1,48,64]{2,1,0:T(8,128)} %shard_map.64) | data formatting | bytes 24576
